TPU v7x, 1024 devices: a whole 8x8x8 slice. The times are simulated.
1024 devices in a mesh: user: 64 (over x, y_hi, core), item: 16 (over y_lo, z).
Axes of the slice: x: 8, y: 8 (y_hi: 4, y_lo: 2; y = y_hi * 2 + y_lo), z: 8, core: 2. Of those that a mesh axis runs over, the one named last changes fastest.
Arguments:
- users: float32 [65536, 256], P(('user', 'item')), may hold values from -1.5 to 1.5
- user_accum: float32 [65536, 256], P(('user', 'item')), may hold values from 0.1 to 10
- items: float32 [262144, 256], P(('user', 'item')), may hold values from -1.5 to 1.5
- item_accum: float32 [262144, 256], P(('user', 'item')), may hold values from 0.1 to 10
- ratings: int32 [2, 65536, 4096], P(None, 'user', 'item'), may hold values from 0 to 1
- tile_mask: int32 [2, 512, 32], P(None, 'user', 'item'), may hold values 0 or 1
Outputs:
- users_out: float32 [65536, 256], P(('user', 'item'))
- items_out: float32 [262144, 256], P(('user', 'item'))
All inputs are finite; a program needn't handle non-finite values. No bound on the sum of `tile_mask` on one device may be relied on, other than what follows from the above.
Results may differ from a plain program's by a relative error of at most 0.013.
Values may be sent and summed in bfloat16 or wider, within the bound.
A program may use at most 32 MiB of HBM per device.

v0:
```python
import jax
import jax.numpy as jnp
from jax import lax
from jax.sharding import PartitionSpec as P


def shifted(array, axis, by):
    count = lax.axis_size(axis)
    return lax.ppermute(array, axis, [(i, (i + by) % count) for i in range(count)])


def adagrad(param, accum, grad):
    accum = accum + grad * grad
    return (param - 0.25 * grad / (jnp.sqrt(accum) + 1e-06), accum)


def expand_mask(mask, rows, cols):
    tile_side = rows // mask.shape[0]
    full = jnp.broadcast_to(
        mask.astype(jnp.float32)[:, None, :, None],
        (mask.shape[0], tile_side, mask.shape[1], tile_side),
    )
    return full.reshape(rows, cols)


def local_grads(user_bf, item_rows, rates, mask):
    item_bf = item_rows.astype(jnp.bfloat16)
    logits = lax.dot_general(
        user_bf, item_bf, (((1,), (1,)), ((), ())), preferred_element_type=jnp.float32
    )
    observed = expand_mask(mask, user_bf.shape[0], item_rows.shape[0])
    errors = (observed * (jax.nn.sigmoid(logits) - rates.astype(jnp.float32))).astype(jnp.bfloat16)
    user_part = jnp.dot(errors, item_bf, preferred_element_type=jnp.float32)
    item_grad = (
        lax.dot_general(
            errors, user_bf, (((0,), (0,)), ((), ())), preferred_element_type=jnp.float32
        )
        + 0.1 * item_rows
    )
    return (user_part, item_grad)


def body(users, user_accum, items, item_accum, ratings, tile_mask):
    strata = ratings.shape[0]
    item_state = jnp.stack((items, item_accum))
    for stratum in range(strata):
        user_bf = lax.all_gather(users.astype(jnp.bfloat16), "item", axis=0, tiled=True)
        user_part, item_grad = local_grads(
            user_bf, item_state[0], ratings[stratum], tile_mask[stratum]
        )
        user_grad = (
            lax.psum_scatter(user_part, "item", scatter_dimension=0, tiled=True) + 0.1 * users
        )
        users, user_accum = adagrad(users, user_accum, user_grad)
        new_items, new_iacc = adagrad(item_state[0], item_state[1], item_grad)
        item_state = jnp.stack((new_items, new_iacc))
        item_state = shifted(item_state, "user", 1)
    item_state = shifted(item_state, "user", -strata)
    return (users, item_state[0])


def solution(mesh):
    return jax.shard_map(
        body,
        mesh=mesh,
        in_specs=(
            P(("user", "item"), None),
            P(("user", "item"), None),
            P(("user", "item"), None),
            P(("user", "item"), None),
            P(None, "user", "item"),
            P(None, "user", "item"),
        ),
        out_specs=(P(("user", "item"), None), P(("user", "item"), None)),
        check_vma=False,
    )
```

profile of v0, /device:TPU:22, one launch (start us, length us, event | category | flops | bytes accessed | tf_op | source)
XLA Modules:
  0.0 276.3 jit_solution(2672679392260307647)
XLA Ops:
  7.2 0.0 reduce-scatter.3.cloned.1.call-start
  7.2 0.7 convert_bitcast_fusion
  7.9 0.1 copy.8
  8.0 0.8 convert_element_type.52
  8.8 47.6 %all_gather.6 = bf16[1024,256]{1,0:T(8,128)(2,1)S(1)} all-gather(bf16[64,256]{1,0:T(8,128)(2,1)S(1)} %convert_element_type.52), channel_id=1, replica_groups=mesh['user'=64,'item'=16] {'item'}, dimensions={0}, use_global_device_ids=true | all-gather | bytes 557056 | tf_op jit(solution)/shard_map/all_gather | solution.py:47
  56.5 0.3 broadcast_in_dim.4
  56.8 0.0 copy-start.1
  56.8 1.8 fusion.10
  58.7 0.0 copy-done.1
  58.7 0.0 copy-start.4
  58.7 1.3 fusion.15
  60.0 0.0 reduce-scatter.3.cloned.1.call-update
  60.0 0.0 copy-start
  60.0 0.0 copy-start.2
  60.0 0.0 reduce-scatter.5.cloned.1.call-start
  60.1 0.0 copy-done.4
  60.1 0.4 subtract_bitcast_fusion.1
  60.5 1.9 collective-permute-start
  62.5 0.1 copy.9
  62.6 72.3 %reduce-scatter.3.cloned.1.call-done = f32[64,256]{1,0:T(8,128)} async-done(((f32[1024,256]{1,0:T(8,128)}), f32[64,256]{1,0:T(8,128)}) %reduce-scatter.3.cloned.1.call-update) | async-done | bytes 65552 | tf_op jit(solution)/shard_map/reduce_scatter | solution.py:52
  134.9 0.0 copy-done
  134.9 0.0 copy-done.2
  134.9 0.9 fusion.22
  135.8 33.4 %all_gather.7 = bf16[1024,256]{1,0:T(8,128)(2,1)S(1)} all-gather(bf16[64,256]{1,0:T(8,128)(2,1)S(1)} %fusion.22), channel_id=1, replica_groups=mesh['user'=64,'item'=16] {'item'}, dimensions={0}, use_global_device_ids=true | all-gather | bytes 557056 | tf_op jit(solution)/shard_map/all_gather | solution.py:47
  169.2 0.0 collective-permute-done
  169.2 0.3 broadcast_in_dim.5
  169.6 1.7 fusion.11
  171.3 1.3 fusion.18
  172.6 0.0 reduce-scatter.5.cloned.1.call-update
  172.6 0.0 copy-start.3
  172.6 0.4 subtract_bitcast_fusion
  173.1 1.9 collective-permute-start.1
  175.0 16.5 %collective-permute-done.1 = f32[2,256,256]{2,1,0:T(8,128)S(1)} collective-permute-done((f32[2,256,256]{2,1,0:T(8,128)S(1)}, f32[2,256,256]{2,1,0:T(8,128)S(1)}, u32[]{:S(2)}, u32[]{:S(2)}) %collective-permute-start.1) | collective-permute-done | bytes 524320 | tf_op jit(solution)/shard_map/ppermute | solution.py:9
  191.5 4.1 %collective-permute-start.2 = (f32[2,256,256]{2,1,0:T(8,128)S(1)}, f32[2,256,256]{2,1,0:T(8,128)S(1)}, u32[]{:S(2)}, u32[]{:S(2)}) collective-permute-start(f32[2,256,256]{2,1,0:T(8,128)S(1)} %collective-permute-done.1), channel_id=1, source_target_pairs={{0,992},{16,1008},{32,0},{48,16},{64,32},{80,48},{96,64},{112,80},... | collective-permute-start | bytes 1572872 | tf_op jit(solution)/shard_map/ppermute | solution.py:9
  195.6 26.8 %collective-permute-done.2 = f32[2,256,256]{2,1,0:T(8,128)S(1)} collective-permute-done((f32[2,256,256]{2,1,0:T(8,128)S(1)}, f32[2,256,256]{2,1,0:T(8,128)S(1)}, u32[]{:S(2)}, u32[]{:S(2)}) %collective-permute-start.2) | collective-permute-done | bytes 524320 | tf_op jit(solution)/shard_map/ppermute | solution.py:9
  222.4 0.7 slice_bitcast_fusion
  223.1 44.8 %reduce-scatter.5.cloned.1.call-done = f32[64,256]{1,0:T(8,128)} async-done(((f32[1024,256]{1,0:T(8,128)}), f32[64,256]{1,0:T(8,128)}) %reduce-scatter.5.cloned.1.call-update) | async-done | bytes 65552 | tf_op jit(solution)/shard_map/reduce_scatter | solution.py:52
  267.9 0.0 copy-done.3
  267.9 1.6 divide_subtract_fusion
  (2 shorter events, 0.1 us)
Async XLA Ops:
  7.2 127.7 %reduce-scatter.3.cloned.1.call-start = ((), (), s32[]{:S(2)}) async-start(), calls=%async_computation.2 | async-start | bytes 1114112 | tf_op jit(solution)/shard_map/reduce_scatter | solution.py:52
  56.8 1.9 copy-start.1
  58.7 1.4 copy-start.4
  60.0 74.9 %copy-start = (f32[64,256]{1,0:T(8,128)S(1)}, f32[64,256]{1,0:T(8,128)}, u32[]{:S(2)}) copy-start(f32[64,256]{1,0:T(8,128)} %param.6) | copy-start | bytes 196612
  60.0 74.9 %copy-start.2 = (f32[64,256]{1,0:T(8,128)S(1)}, f32[64,256]{1,0:T(8,128)}, u32[]{:S(2)}) copy-start(f32[64,256]{1,0:T(8,128)} %param.7) | copy-start | bytes 196612
  60.0 207.9 %reduce-scatter.5.cloned.1.call-start = ((), (), s32[]{:S(2)}) async-start(), calls=%async_computation.3 | async-start | bytes 1114112 | tf_op jit(solution)/shard_map/reduce_scatter | solution.py:52
  60.5 108.7 %collective-permute-start = (f32[2,256,256]{2,1,0:T(8,128)S(1)}, f32[2,256,256]{2,1,0:T(8,128)S(1)}, u32[]{:S(2)}, u32[]{:S(2)}) collective-permute-start(f32[2,256,256]{2,1,0:T(8,128)S(1)} %pad_maximum_fusion), channel_id=1, source_target_pairs={{0,16},{16,32},{32,48},{48,64},{64,80},{80,96},{96,112},{112,128},... | collective-permute-start | bytes 1572872 | tf_op jit(solution)/shard_map/ppermute | solution.py:9
  172.6 95.3 %copy-start.3 = (f32[64,256]{1,0:T(8,128)S(1)}, f32[64,256]{1,0:T(8,128)}, u32[]{:S(2)}) copy-start(f32[64,256]{1,0:T(8,128)} %reduce-scatter.3.cloned.1.call-done) | copy-start | bytes 196612
  173.1 18.5 %collective-permute-start.1 = (f32[2,256,256]{2,1,0:T(8,128)S(1)}, f32[2,256,256]{2,1,0:T(8,128)S(1)}, u32[]{:S(2)}, u32[]{:S(2)}) collective-permute-start(f32[2,256,256]{2,1,0:T(8,128)S(1)} %pad_maximum_fusion.1), channel_id=1, source_target_pairs={{0,16},{16,32},{32,48},{48,64},{64,80},{80,96},{96,112},{112,128},... | collective-permute-start | bytes 1572872 | tf_op jit(solution)/shard_map/ppermute | solution.py:9
  191.5 30.8 %collective-permute-start.2 = (f32[2,256,256]{2,1,0:T(8,128)S(1)}, f32[2,256,256]{2,1,0:T(8,128)S(1)}, u32[]{:S(2)}, u32[]{:S(2)}) collective-permute-start(f32[2,256,256]{2,1,0:T(8,128)S(1)} %collective-permute-done.1), channel_id=1, source_target_pairs={{0,992},{16,1008},{32,0},{48,16},{64,32},{80,48},{96,64},{112,80},... | collective-permute-start | bytes 1572872 | tf_op jit(solution)/shard_map/ppermute | solution.py:9
Sparse Core Ops, SparseCore 0:
  60.1 74.7 reduce-scatter.2
  172.7 95.1 reduce-scatter.4
where the time goes:
time: 277 us; the launch traced here: 276 us
  waiting for transfers between devices  161 us (58%)
  blocking collectives  81.1 us (29%)
  between operations  14.2 us (5%)
  starting transfers between devices  7.98 us (3%)
  matrix products  6.93 us (3%)
  other arithmetic  4.06 us (1%)
    reduce_scatter x2, waiting for transfers between devices, body(): lax.psum_scatter(user_part, 'item', scatter_dimension=0, tiled=True)  117 us
    all_gather x2, blocking collectives, body(): lax.all_gather(users.astype(jnp.bfloat16), 'item', axis=0, tiled=True)  81.1 us
    ppermute x3, waiting for transfers between devices, shifted(): lax.ppermute(array, axis, [(i, (i + by) % count) for i in range(count)])  43.3 us
    ppermute x3, starting transfers between devices, shifted(): lax.ppermute(array, axis, [(i, (i + by) % count) for i in range(count)])  7.9 us
  transfers between devices with their start and end apart: 5, of which 4 were waited for; matrix products, arithmetic and copies ran while one was open for 1% of the time, Pallas kernels for 0%

commit v1 on v0

v1 whole, which is shorter than its diff:
```python
import functools
import math

import jax
import jax.numpy as jnp
from jax import lax
from jax.experimental import pallas as pl
from jax.experimental.pallas import tpu as pltpu
from jax.sharding import PartitionSpec as P

MESH = pl.DeviceIdType.MESH
RING = 8

NODES = (
    (0, 0, None),
    (0, 2, 0),
    (0, -2, 0),
    (1, 0, 0),
    (0, 1, 0),
    (0, -1, 0),
    (0, 4, 1),
    (1, 2, 1),
    (0, 3, 1),
    (1, -2, 2),
    (0, -3, 2),
    (1, 1, 3),
    (1, -1, 3),
    (1, 4, 6),
    (1, 3, 7),
    (1, -3, 9),
)
GROUPS = ((0, 6), (6, 13), (13, 16))


FLOOR, TOP = 1 / 16, 8192.0
STEPS = 32767 / math.log(1 + TOP / FLOOR)


def encode(x):
    steps = jnp.minimum(STEPS * jnp.log(1.0 + jnp.abs(x) * (1 / FLOOR)) + 0.5, 32767.0)
    return jnp.where(x < 0, -steps, steps).astype(jnp.int32).astype(jnp.int16)


def decode(code):
    steps = code.astype(jnp.int32).astype(jnp.float32)
    size = FLOOR * jnp.exp(jnp.abs(steps) * (1 / STEPS)) - FLOOR
    return jnp.where(steps < 0, -size, size)


def children_of(node):
    return [n for n, row in enumerate(NODES) if row[2] == node]


def hop(start, end):
    return (NODES[end][0] - NODES[start][0]) % 2, NODES[end][1] - NODES[start][1]


def peers():
    found = set()
    for node, row in enumerate(NODES):
        if row[2] is not None:
            dy, dz = hop(row[2], node)
            found |= {(dy, dz % RING), (dy, -dz % RING)}
    return sorted(found)


def adagrad(param, accum, grad):
    accum = accum + grad * grad
    return param - 0.25 * grad / (jnp.sqrt(accum) + 1e-06), accum


def kernel(
    n_user, users_h, uacc_h, items_h, iacc_h, rates_h, mask_h, users_o, items_o,
    rates, mask, user_v, uacc_v, item_v, iacc_v, item_b, gather, errors, parts, outgo, income, grad_out, grad_in,
    load_sem, gs_send, gs_recv, rs_send, rs_recv, it_send, it_recv,
):
    f32, bf16 = jnp.float32, jnp.bfloat16
    strata = rates_h.shape[0]
    rows = users_h.shape[0]
    cols = items_h.shape[0]
    tile_rows = len(NODES) * rows // mask_h.shape[2]
    tile_cols = cols // mask_h.shape[1]
    u, i = lax.axis_index("user"), lax.axis_index("item")
    y, z = i // RING, i % RING
    after, before = (u + 1) % n_user, (u + n_user - 1) % n_user

    loads = [
        (users_h, user_v), (items_h, item_v), (mask_h, mask), (rates_h.at[0], rates.at[0]),
        (iacc_h, iacc_v), (uacc_h, uacc_v), (rates_h.at[1], rates.at[1]),
    ]
    loads = [pltpu.make_async_copy(src, dst, load_sem.at[k]) for k, (src, dst) in enumerate(loads)]
    for load in loads:
        load.start()

    barrier = pltpu.get_barrier_semaphore()
    near = peers()
    for dy, dz in near:
        there = (u, ((y + dy) % 2) * RING + (z + dz) % RING)
        pl.semaphore_signal(barrier, inc=1, device_id=there, device_id_type=MESH)
    for v in (after, before):
        pl.semaphore_signal(barrier, inc=1, device_id=(v, i), device_id_type=MESH)

    def side(node):
        return 1 - 2 * ((z + NODES[node][1] + RING) % 2)

    def owner(node):
        dy, dz, _ = NODES[node]
        return ((y + dy) % 2) * RING + (z - side(node) * dz + RING) % RING

    def target(start, end):
        dy, dz = hop(start, end)
        return (u, ((y + dy) % 2) * RING + (z + side(start) * dz + RING) % RING)

    def block(node):
        return pl.ds(node * rows, rows)

    def down(s, node, child):
        return pltpu.make_async_remote_copy(
            src_ref=gather.at[s, block(node)], dst_ref=gather.at[s, block(child)],
            send_sem=gs_send.at[s, child], recv_sem=gs_recv.at[s, child],
            device_id=target(node, child), device_id_type=MESH,
        )

    def up(s, node):
        return pltpu.make_async_remote_copy(
            src_ref=outgo.at[s, block(node)], dst_ref=income.at[s, block(node)],
            send_sem=rs_send.at[s, node], recv_sem=rs_recv.at[s, node],
            device_id=target(node, NODES[node][2]), device_id_type=MESH,
        )

    items_on = pltpu.make_async_remote_copy(
        src_ref=item_b.at[2], dst_ref=item_b.at[1], send_sem=it_send.at[0], recv_sem=it_recv.at[0],
        device_id=(after, i), device_id_type=MESH,
    )
    grads_back = pltpu.make_async_remote_copy(
        src_ref=grad_out, dst_ref=grad_in, send_sem=it_send.at[1], recv_sem=it_recv.at[1],
        device_id=(before, i), device_id_type=MESH,
    )

    def compute(s, first, last):
        item_rows = item_b[s]
        span = slice(first * rows, last * rows)
        logits = lax.dot_general(
            gather[s, span, :], item_rows, (((1,), (1,)), ((), ())), preferred_element_type=f32
        )
        half = 0.5 * jnp.tanh(0.5 * logits) + 0.5
        for node in range(first, last):
            own = owner(node)
            at = pl.ds(pl.multiple_of(own * rows, rows), rows)
            mine = half[(node - first) * rows : (node - first + 1) * rows]
            wrong = mine - rates[s, at, :].astype(f32)
            for t in range(cols // tile_cols):
                seen = mask[s, t, own * rows // tile_rows].astype(f32)
                c = slice(t * tile_cols, (t + 1) * tile_cols)
                errors[block(node), c] = (seen * wrong[:, c]).astype(bf16)
        share = jnp.dot(errors[span, :], item_rows, preferred_element_type=f32)
        for node in range(first, last):
            mine = share[(node - first) * rows : (node - first + 1) * rows]
            if node > 0 and not children_of(node):
                outgo[s, block(node), :] = encode(mine)
                up(s, node).start()
            else:
                parts[block(node), :] = mine

    loads[0].wait()
    gather[0, block(0), :] = user_v[...].astype(bf16)
    pl.semaphore_wait(barrier, len(near) + 2)

    for s in range(strata):
        for child in children_of(0):
            down(s, 0, child).start()
        if s == 0:
            loads[1].wait()
            item_b[0] = item_v[...].astype(bf16)
            loads[2].wait()
            loads[3].wait()
        else:
            loads[6].wait()
            items_on.wait_recv()
        for first, last in GROUPS:
            for node in range(max(first, 1), last):
                down(s, NODES[node][2], node).wait_recv()
                for child in children_of(node):
                    down(s, node, child).start()
            compute(s, first, last)

        item_grad = lax.dot_general(
            errors[...], gather[s], (((0,), (0,)), ((), ())), preferred_element_type=f32
        )
        if s == 0:
            loads[4].wait()
            new_items, new_iacc = adagrad(item_v[...], iacc_v[...], item_grad + 0.1 * item_v[...])
            item_v[...] = new_items
            iacc_v[...] = new_iacc
            item_b[2] = new_items.astype(bf16)
            items_on.start()
        else:
            grad_out[...] = item_grad.astype(bf16)
            grads_back.start()

        for node in reversed(range(len(NODES))):
            below = children_of(node)
            if not below:
                continue
            total = parts[block(node), :]
            for child in below:
                up(s, child).wait_recv()
                total = total + decode(income[s, block(child), :])
            if node > 0:
                outgo[s, block(node), :] = encode(total)
                up(s, node).start()
        if s == 0:
            loads[5].wait()
        new_users, new_uacc = adagrad(user_v[...], uacc_v[...], total + 0.1 * user_v[...])
        if s == 0:
            user_v[...] = new_users
            uacc_v[...] = new_uacc
            gather[1, block(0), :] = new_users.astype(bf16)
        else:
            users_o[...] = new_users

    grads_back.wait_recv()
    new_items, _ = adagrad(
        item_v[...], iacc_v[...], grad_in[...].astype(f32) + 0.1 * item_v[...]
    )
    items_o[...] = new_items

    items_on.wait_send()
    grads_back.wait_send()
    for s in range(strata):
        for node in range(1, len(NODES)):
            down(s, NODES[node][2], node).wait_send()
            up(s, node).wait_send()


def solution(mesh):
    n_user = mesh.shape["user"]
    count = len(NODES)

    def body(users, user_accum, items, item_accum, ratings, tile_mask):
        f32, bf16 = jnp.float32, jnp.bfloat16
        tile_mask = jnp.swapaxes(tile_mask, 1, 2)
        rows, rank = users.shape
        cols = items.shape[0]
        whole = count * rows
        sems = pltpu.SemaphoreType.DMA((2, count))
        return pl.pallas_call(
            functools.partial(kernel, n_user),
            out_shape=(
                jax.ShapeDtypeStruct((rows, rank), f32),
                jax.ShapeDtypeStruct((cols, rank), f32),
            ),
            in_specs=[pl.BlockSpec(memory_space=pl.ANY)] * 6,
            out_specs=(pl.BlockSpec(memory_space=pltpu.VMEM),) * 2,
            scratch_shapes=[
                pltpu.VMEM((2, whole, cols), jnp.int32),
                pltpu.SMEM(tile_mask.shape, jnp.int32),
                pltpu.VMEM((rows, rank), f32),
                pltpu.VMEM((rows, rank), f32),
                pltpu.VMEM((cols, rank), f32),
                pltpu.VMEM((cols, rank), f32),
                pltpu.VMEM((3, cols, rank), bf16),
                pltpu.VMEM((2, whole, rank), bf16),
                pltpu.VMEM((whole, cols), bf16),
                pltpu.VMEM((whole, rank), f32),
                pltpu.VMEM((2, whole, rank), jnp.int16),
                pltpu.VMEM((2, whole, rank), jnp.int16),
                pltpu.VMEM((cols, rank), bf16),
                pltpu.VMEM((cols, rank), bf16),
                pltpu.SemaphoreType.DMA((7,)),
                sems,
                sems,
                sems,
                sems,
                pltpu.SemaphoreType.DMA((2,)),
                pltpu.SemaphoreType.DMA((2,)),
            ],
            compiler_params=pltpu.CompilerParams(
                collective_id=0, has_side_effects=True, vmem_limit_bytes=56 * 2**20
            ),
        )(users, user_accum, items, item_accum, ratings, tile_mask)

    return jax.shard_map(
        body,
        mesh=mesh,
        in_specs=(
            P(("user", "item"), None),
            P(("user", "item"), None),
            P(("user", "item"), None),
            P(("user", "item"), None),
            P(None, "user", "item"),
            P(None, "user", "item"),
        ),
        out_specs=(P(("user", "item"), None), P(("user", "item"), None)),
        check_vma=False,
    )
```

time: 277 us -> 72.9 us (0.26)
  the two profiles are of different devices: /device:TPU:22 before, /device:TPU:14 now
where the time goes in v1:
time: 72.9 us; the launch traced here: 72.7 us
  Pallas kernels  68.9 us (95%)
  local copies, waits for them, and re-layouts  3.14 us (4%)
    pallas_call x1, Pallas kernels, body(): pl.pallas_call(functools.partial(kernel, n_user), out_shape=(jax.ShapeDty...  68.9 us
    unnamed x2, local copies, waits for them, and re-layouts  3.14 us

profile of v1, /device:TPU:14, one launch (start us, length us, event | category | flops | bytes accessed | tf_op | source)
XLA Modules:
  0.0 72.7 jit_solution(12883772104503333216)
XLA Ops:
  0.6 68.9 %shard_map.77 = (f32[64,256]{1,0:T(8,128)}, f32[256,256]{1,0:T(8,128)}) custom-call(f32[64,256]{1,0:T(8,128)} %users_h.1, f32[64,256]{1,0:T(8,128)} %uacc_h.1, f32[256,256]{1,0:T(8,128)} %items_h.1, f32[256,256]{1,0:T(8,128)} %iacc_h.1, s32[2,1024,256]{2,1,0:T(8,128)} %rates_h.1, s32[2,2,8]{2,1,0:T(2,128)} %bitcast.1), custom_call_target="tpu_custom_call" | custom-call | tf_op jit(solution)/shard_map/pallas_call | solution.py:247
  69.5 1.5 %copy.10 = f32[64,256]{1,0:T(8,128)} copy(f32[64,256]{1,0:T(8,128)} %get-tuple-element.4) | data formatting | bytes 131072
  71.0 1.7 %copy.11 = f32[256,256]{1,0:T(8,128)} copy(f32[256,256]{1,0:T(8,128)} %get-tuple-element.5) | data formatting | bytes 524288

commit v2 on v0

v2 whole, which is shorter than its diff:
```python
import functools
import math

import jax
import jax.numpy as jnp
from jax import lax
from jax.experimental import pallas as pl
from jax.experimental.pallas import tpu as pltpu
from jax.sharding import PartitionSpec as P

MESH = pl.DeviceIdType.MESH
RING = 8
OFFSETS = (0, 1, -1, 2, -2, 3, -3, 4)
GROUPS = ((0, 3), (3, 5), (5, 8))
SENDS = (7, 6, 5, 4, 3, 2, 1)

FLOOR, TOP = 1 / 16, 8192.0
STEPS = 32767 / math.log(1 + TOP / FLOOR)


def encode(x):
    steps = jnp.minimum(STEPS * jnp.log(1.0 + jnp.abs(x) * (1 / FLOOR)) + 0.5, 32767.0)
    return jnp.where(x < 0, -steps, steps).astype(jnp.int32).astype(jnp.int16)


def decode(code):
    steps = code.astype(jnp.int32).astype(jnp.float32)
    size = FLOOR * jnp.exp(jnp.abs(steps) * (1 / STEPS)) - FLOOR
    return jnp.where(steps < 0, -size, size)


def adagrad(param, accum, grad):
    accum = accum + grad * grad
    return param - 0.25 * grad / (jnp.sqrt(accum) + 1e-06), accum


def kernel(
    n_user, users_h, uacc_h, items_h, iacc_h, rates_h, mask_h, users_o, items_o,
    rates, rates_p, rates_out, rates_in, mask, mask_v, mask_p, user_v, uacc_v, item_v, iacc_v,
    item_b, item_new, gather, errors, part, outgo, income, grad_out, grad_in,
    load_sem, gs_send, gs_recv, rs_send, rs_recv, y_send, y_recv, it_send, it_recv,
):
    f32, bf16 = jnp.float32, jnp.bfloat16
    strata = rates_h.shape[0]
    rows, cols = users_h.shape[0], items_h.shape[0]
    plane = RING * rows
    tile_rows = 2 * plane // mask_h.shape[2]
    tile_cols = cols // mask_h.shape[1]
    u, i = lax.axis_index("user"), lax.axis_index("item")
    y, z = i // RING, i % RING
    across = (1 - y) * RING + z
    after, before = (u + 1) % n_user, (u + n_user - 1) % n_user

    def forth(k):
        return (u, y * RING + (z + OFFSETS[k] + RING) % RING)

    def place(k):
        return (z - OFFSETS[k] + RING) % RING

    def back(k):
        return (u, y * RING + place(k))

    def slot(k):
        return pl.ds(k * rows, rows)

    def half(s, p):
        return rates_h.at[s, pl.ds(pl.multiple_of(p * plane, plane), plane)]

    loads = [
        (users_h, user_v), (half(0, 1 - y), rates_p.at[0]), (items_h, item_v), (mask_h, mask.at[pl.ds(0, strata)]), (mask_h, mask_v),
        (half(0, y), rates.at[0]), (half(1, 1 - y), rates_p.at[1]), (iacc_h, iacc_v), (uacc_h, uacc_v),
        (half(1, y), rates.at[1]),
    ]
    loads = [pltpu.make_async_copy(src, dst, load_sem.at[k]) for k, (src, dst) in enumerate(loads)]
    for load in loads:
        load.start()

    near = [forth(k) for k in range(1, RING)] + [(v, j) for v in (after, before) for j in (i, across)] + [(u, across)]
    barrier = pltpu.get_barrier_semaphore()
    for there in near:
        pl.semaphore_signal(barrier, inc=1, device_id=there, device_id_type=MESH)

    def copy(src, dst, send, recv, there):
        return pltpu.make_async_remote_copy(
            src_ref=src, dst_ref=dst, send_sem=send, recv_sem=recv, device_id=there, device_id_type=MESH
        )

    def spread(s, k):
        return copy(gather.at[s, slot(0)], gather.at[s, slot(k)], gs_send.at[s, k], gs_recv.at[s, k], forth(k))

    def collect(s, k):
        return copy(outgo.at[s, slot(k)], income.at[s, slot(k)], rs_send.at[s, k], rs_recv.at[s, k], back(k))

    def to_partner(k, src, dst):
        return copy(src, dst, y_send.at[k], y_recv.at[k], (u, across))

    swap_items = to_partner(0, item_b.at[0, pl.ds(0, cols)], item_b.at[0, pl.ds(cols, cols)])
    swap_mask = to_partner(1, mask_v, mask_p)
    swap_grad = to_partner(2, grad_out.at[2], grad_in.at[2])
    swap_late = to_partner(3, rates_out.at[1], rates_in.at[1])
    swap_rates = []
    for n, (first, last) in enumerate(GROUPS):
        span = pl.ds(first * rows, (last - first) * rows)
        swap_rates.append(to_partner(4 + n, rates_out.at[0, span], rates_in.at[0, span]))
    items_on = [
        copy(item_new, item_b.at[1, pl.ds(n * cols, cols)], it_send.at[n], it_recv.at[n], (after, j))
        for n, j in enumerate((i, across))
    ]
    grads_back = [
        copy(grad_out.at[n], grad_in.at[n], it_send.at[2 + n], it_recv.at[2 + n], (before, j))
        for n, j in enumerate((i, across))
    ]

    def pack_rates(s):
        for k in range(RING):
            at = pl.ds(pl.multiple_of(place(k) * rows, rows), rows)
            rates_out[s, slot(k), :] = rates_p[s, at, :].astype(f32).astype(bf16)

    def compute(s, first, last):
        span = slice(first * rows, last * rows)
        item_rows = item_b[s]
        logits = lax.dot_general(
            gather[s, span, :], item_rows, (((1,), (1,)), ((), ())), preferred_element_type=f32
        )
        likely = 0.5 * jnp.tanh(0.5 * logits) + 0.5
        for k in range(first, last):
            at = pl.ds(pl.multiple_of(place(k) * rows, rows), rows)
            tile = (y * plane + place(k) * rows) // tile_rows
            mine = likely[(k - first) * rows : (k - first + 1) * rows]
            for h in range(2):
                rate = rates[s, at, :].astype(f32) if h == 0 else rates_in[s, slot(k), :].astype(f32)
                base = s + h * strata
                wrong = mine[:, h * cols : (h + 1) * cols] - rate
                for t in range(cols // tile_cols):
                    weight = mask[base, t, tile].astype(f32)
                    c = h * cols + t * tile_cols
                    errors[slot(k), c : c + tile_cols] = (
                        weight * wrong[:, t * tile_cols : (t + 1) * tile_cols]
                    ).astype(bf16)
        share = jnp.dot(errors[span, :], item_rows, preferred_element_type=f32)
        for k in range(first, last):
            mine = share[(k - first) * rows : (k - first + 1) * rows]
            if k > 0:
                outgo[s, slot(k), :] = encode(mine)
                collect(s, k).start()
            else:
                part[...] = mine

    def item_sum(s, h):
        return lax.dot_general(
            errors[:, h * cols : (h + 1) * cols], gather[s], (((0,), (0,)), ((), ())), preferred_element_type=f32
        )

    mask_s = mask.at[pl.ds(strata, strata)]
    loads[0].wait()
    gather[0, slot(0), :] = user_v[...].astype(bf16)
    loads[2].wait()
    item_b[0, pl.ds(0, cols), :] = item_v[...].astype(bf16)
    loads[1].wait()
    pack_rates(0)
    loads[4].wait()
    pl.semaphore_wait(barrier, len(near))

    for s in range(strata):
        for k in SENDS:
            spread(s, k).start()
        if s == 0:
            swap_items.start()
            swap_mask.start()
            for swap in swap_rates:
                swap.start()
            loads[6].wait()
            pack_rates(1)
            loads[3].wait()
            loads[5].wait()
            swap_mask.wait_recv()
            local = pltpu.make_async_copy(mask_p, mask_s, load_sem.at[10])
            local.start()
            local.wait()
            swap_items.wait_recv()
        else:
            loads[9].wait()
            swap_late.wait_recv()
            for on in items_on:
                on.wait_recv()
        for n, (first, last) in enumerate(GROUPS):
            for k in range(max(first, 1), last):
                spread(s, k).wait_recv()
            if s == 0:
                swap_rates[n].wait_recv()
            compute(s, first, last)

        if s == 0:
            grad_out[2] = item_sum(s, 1).astype(bf16)
            swap_grad.start()
            swap_late.start()
            item_grad = item_sum(s, 0)
            loads[7].wait()
            swap_grad.wait_recv()
            item_grad = item_grad + grad_in[2].astype(f32) + 0.1 * item_v[...]
            new_items, new_iacc = adagrad(item_v[...], iacc_v[...], item_grad)
            item_v[...] = new_items
            iacc_v[...] = new_iacc
            item_new[...] = new_items.astype(bf16)
            for on in items_on:
                on.start()
        else:
            for n in range(2):
                grad_out[n] = item_sum(s, n).astype(bf16)
                grads_back[n].start()

        total = part[...] + 0.1 * user_v[...]
        for k in range(1, RING):
            collect(s, k).wait_recv()
            total = total + decode(income[s, slot(k), :])
        if s == 0:
            loads[8].wait()
        new_users, new_uacc = adagrad(user_v[...], uacc_v[...], total)
        if s == 0:
            user_v[...] = new_users
            uacc_v[...] = new_uacc
            gather[1, slot(0), :] = new_users.astype(bf16)
        else:
            users_o[...] = new_users

    for grads in grads_back:
        grads.wait_recv()
    item_grad = grad_in[0].astype(f32) + grad_in[1].astype(f32) + 0.1 * item_v[...]
    new_items, _ = adagrad(item_v[...], iacc_v[...], item_grad)
    items_o[...] = new_items

    for sent in [swap_items, swap_mask, swap_grad, swap_late, *swap_rates, *items_on, *grads_back]:
        sent.wait_send()
    for s in range(strata):
        for k in range(1, RING):
            spread(s, k).wait_send()
            collect(s, k).wait_send()


def solution(mesh):
    n_user = mesh.shape["user"]

    def body(users, user_accum, items, item_accum, ratings, tile_mask):
        f32, bf16, i32 = jnp.float32, jnp.bfloat16, jnp.int32
        tile_mask = jnp.swapaxes(tile_mask, 1, 2)
        strata = ratings.shape[0]
        rows, rank = users.shape
        cols = items.shape[0]
        plane = RING * rows
        ring_sems = pltpu.SemaphoreType.DMA((strata, RING))
        return pl.pallas_call(
            functools.partial(kernel, n_user),
            out_shape=(
                jax.ShapeDtypeStruct((rows, rank), f32),
                jax.ShapeDtypeStruct((cols, rank), f32),
            ),
            in_specs=[pl.BlockSpec(memory_space=pl.ANY)] * 6,
            out_specs=(pl.BlockSpec(memory_space=pltpu.VMEM),) * 2,
            scratch_shapes=[
                pltpu.VMEM((strata, plane, cols), i32),
                pltpu.VMEM((strata, plane, cols), i32),
                pltpu.VMEM((strata, plane, cols), bf16),
                pltpu.VMEM((strata, plane, cols), bf16),
                pltpu.SMEM((2 * strata, *tile_mask.shape[1:]), i32),
                pltpu.VMEM(tile_mask.shape, i32),
                pltpu.VMEM(tile_mask.shape, i32),
                pltpu.VMEM((rows, rank), f32),
                pltpu.VMEM((rows, rank), f32),
                pltpu.VMEM((cols, rank), f32),
                pltpu.VMEM((cols, rank), f32),
                pltpu.VMEM((strata, 2 * cols, rank), bf16),
                pltpu.VMEM((cols, rank), bf16),
                pltpu.VMEM((strata, plane, rank), bf16),
                pltpu.VMEM((plane, 2 * cols), bf16),
                pltpu.VMEM((rows, rank), f32),
                pltpu.VMEM((strata, plane, rank), jnp.int16),
                pltpu.VMEM((strata, plane, rank), jnp.int16),
                pltpu.VMEM((3, cols, rank), bf16),
                pltpu.VMEM((3, cols, rank), bf16),
                pltpu.SemaphoreType.DMA((11,)),
                ring_sems,
                ring_sems,
                ring_sems,
                ring_sems,
                pltpu.SemaphoreType.DMA((4 + len(GROUPS),)),
                pltpu.SemaphoreType.DMA((4 + len(GROUPS),)),
                pltpu.SemaphoreType.DMA((4,)),
                pltpu.SemaphoreType.DMA((4,)),
            ],
            compiler_params=pltpu.CompilerParams(
                collective_id=0, has_side_effects=True, vmem_limit_bytes=56 * 2**20
            ),
        )(users, user_accum, items, item_accum, ratings, tile_mask)

    return jax.shard_map(
        body,
        mesh=mesh,
        in_specs=(
            P(("user", "item"), None),
            P(("user", "item"), None),
            P(("user", "item"), None),
            P(("user", "item"), None),
            P(None, "user", "item"),
            P(None, "user", "item"),
        ),
        out_specs=(P(("user", "item"), None), P(("user", "item"), None)),
        check_vma=False,
    )
```

time: 277 us -> 62.8 us (0.23)
  the two profiles are of different devices: /device:TPU:22 before, /device:TPU:9 now
where the time goes in v2:
time: 62.8 us; the launch traced here: 62.5 us
  Pallas kernels  58.7 us (93%)
  local copies, waits for them, and re-layouts  3.14 us (5%)
  between operations  0.64 us (1%)
    pallas_call x1, Pallas kernels, body(): pl.pallas_call(functools.partial(kernel, n_user), out_shape=(jax.ShapeDty...  58.7 us
    unnamed x2, local copies, waits for them, and re-layouts  3.14 us

profile of v2, /device:TPU:9, one launch (start us, length us, event | category | flops | bytes accessed | tf_op | source)
XLA Modules:
  0.0 62.5 jit_solution(17526614267329294965)
XLA Ops:
  0.6 58.7 %shard_map.77 = (f32[64,256]{1,0:T(8,128)}, f32[256,256]{1,0:T(8,128)}) custom-call(f32[64,256]{1,0:T(8,128)} %users_h.1, f32[64,256]{1,0:T(8,128)} %uacc_h.1, f32[256,256]{1,0:T(8,128)} %items_h.1, f32[256,256]{1,0:T(8,128)} %iacc_h.1, s32[2,1024,256]{2,1,0:T(8,128)} %rates_h.1, s32[2,2,8]{2,1,0:T(2,128)} %bitcast.1), custom_call_target="tpu_custom_call" | custom-call | tf_op jit(solution)/shard_map/pallas_call | solution.py:251
  59.4 1.5 %copy.10 = f32[64,256]{1,0:T(8,128)} copy(f32[64,256]{1,0:T(8,128)} %get-tuple-element.4) | data formatting | bytes 131072
  60.9 1.7 %copy.11 = f32[256,256]{1,0:T(8,128)} copy(f32[256,256]{1,0:T(8,128)} %get-tuple-element.5) | data formatting | bytes 524288

commit v3 on v2

--- a/solution.py
+++ b/solution.py
@@ -10,9 +10,10 @@
 
 MESH = pl.DeviceIdType.MESH
 RING = 8
-OFFSETS = (0, 1, -1, 2, -2, 3, -3, 4)
-GROUPS = ((0, 3), (3, 5), (5, 8))
-SENDS = (7, 6, 5, 4, 3, 2, 1)
+OFFSETS = (0, 4, 3, -3, 2, -2, 1, -1)
+GROUPS = ((0, 2), (2, 4), (4, 6), (6, 8))
+SHARES = ((0, 4), (4, 8))
+SENDS = (1, 2, 3, 4, 5, 6, 7)
 
 FLOOR, TOP = 1 / 16, 8192.0
 STEPS = 32767 / math.log(1 + TOP / FLOOR)
@@ -37,7 +38,7 @@
 def kernel(
     n_user, users_h, uacc_h, items_h, iacc_h, rates_h, mask_h, users_o, items_o,
     rates, rates_p, rates_out, rates_in, mask, mask_v, mask_p, user_v, uacc_v, item_v, iacc_v,
-    item_b, item_new, gather, errors, part, outgo, income, grad_out, grad_in,
+    item_b, item_new, item_grad, gather, errors, part, outgo, income, grad_out, grad_in,
     load_sem, gs_send, gs_recv, rs_send, rs_recv, y_send, y_recv, it_send, it_recv,
 ):
     f32, bf16 = jnp.float32, jnp.bfloat16
@@ -116,28 +117,28 @@
             at = pl.ds(pl.multiple_of(place(k) * rows, rows), rows)
             rates_out[s, slot(k), :] = rates_p[s, at, :].astype(f32).astype(bf16)
 
-    def compute(s, first, last):
+    def compute(s, h, first, last):
         span = slice(first * rows, last * rows)
-        item_rows = item_b[s]
         logits = lax.dot_general(
-            gather[s, span, :], item_rows, (((1,), (1,)), ((), ())), preferred_element_type=f32
+            gather[s, span, :], item_b[s, h * cols : (h + 1) * cols, :], (((1,), (1,)), ((), ())),
+            preferred_element_type=f32,
         )
         likely = 0.5 * jnp.tanh(0.5 * logits) + 0.5
         for k in range(first, last):
             at = pl.ds(pl.multiple_of(place(k) * rows, rows), rows)
             tile = (y * plane + place(k) * rows) // tile_rows
-            mine = likely[(k - first) * rows : (k - first + 1) * rows]
-            for h in range(2):
-                rate = rates[s, at, :].astype(f32) if h == 0 else rates_in[s, slot(k), :].astype(f32)
-                base = s + h * strata
-                wrong = mine[:, h * cols : (h + 1) * cols] - rate
-                for t in range(cols // tile_cols):
-                    weight = mask[base, t, tile].astype(f32)
-                    c = h * cols + t * tile_cols
-                    errors[slot(k), c : c + tile_cols] = (
-                        weight * wrong[:, t * tile_cols : (t + 1) * tile_cols]
-                    ).astype(bf16)
-        share = jnp.dot(errors[span, :], item_rows, preferred_element_type=f32)
+            rate = rates[s, at, :].astype(f32) if h == 0 else rates_in[s, slot(k), :].astype(f32)
+            wrong = likely[(k - first) * rows : (k - first + 1) * rows] - rate
+            for t in range(cols // tile_cols):
+                weight = mask[s + h * strata, t, tile].astype(f32)
+                c = slice(t * tile_cols, (t + 1) * tile_cols)
+                errors[slot(k), h * cols + t * tile_cols : h * cols + (t + 1) * tile_cols] = (
+                    weight * wrong[:, c]
+                ).astype(bf16)
+
+    def share_out(s, first, last):
+        span = slice(first * rows, last * rows)
+        share = jnp.dot(errors[span, :], item_b[s], preferred_element_type=f32)
         for k in range(first, last):
             mine = share[(k - first) * rows : (k - first + 1) * rows]
             if k > 0:
@@ -165,49 +166,60 @@
         for k in SENDS:
             spread(s, k).start()
         if s == 0:
+            swap_mask.start()
             swap_items.start()
-            swap_mask.start()
             for swap in swap_rates:
                 swap.start()
             loads[6].wait()
             pack_rates(1)
             loads[3].wait()
             loads[5].wait()
+        else:
+            loads[9].wait()
+            items_on[0].wait_recv()
+        for first, last in GROUPS:
+            for k in range(max(first, 1), last):
+                spread(s, k).wait_recv()
+            compute(s, 0, first, last)
+        if s == 0:
+            item_grad[...] = item_sum(s, 0)
             swap_mask.wait_recv()
             local = pltpu.make_async_copy(mask_p, mask_s, load_sem.at[10])
             local.start()
             local.wait()
             swap_items.wait_recv()
         else:
-            loads[9].wait()
+            grad_out[0] = item_sum(s, 0).astype(bf16)
+            grads_back[0].start()
             swap_late.wait_recv()
-            for on in items_on:
-                on.wait_recv()
+            items_on[1].wait_recv()
         for n, (first, last) in enumerate(GROUPS):
-            for k in range(max(first, 1), last):
-                spread(s, k).wait_recv()
             if s == 0:
                 swap_rates[n].wait_recv()
-            compute(s, first, last)
-
+            compute(s, 1, first, last)
+            if s == 0:
+                share_out(s, first, last)
         if s == 0:
             grad_out[2] = item_sum(s, 1).astype(bf16)
             swap_grad.start()
             swap_late.start()
-            item_grad = item_sum(s, 0)
+        else:
+            grad_out[1] = item_sum(s, 1).astype(bf16)
+            grads_back[1].start()
+        if s > 0:
+            for first, last in SHARES:
+                share_out(s, first, last)
+
+        if s == 0:
             loads[7].wait()
             swap_grad.wait_recv()
-            item_grad = item_grad + grad_in[2].astype(f32) + 0.1 * item_v[...]
-            new_items, new_iacc = adagrad(item_v[...], iacc_v[...], item_grad)
+            whole = item_grad[...] + grad_in[2].astype(f32) + 0.1 * item_v[...]
+            new_items, new_iacc = adagrad(item_v[...], iacc_v[...], whole)
             item_v[...] = new_items
             iacc_v[...] = new_iacc
             item_new[...] = new_items.astype(bf16)
             for on in items_on:
                 on.start()
-        else:
-            for n in range(2):
-                grad_out[n] = item_sum(s, n).astype(bf16)
-                grads_back[n].start()
 
         total = part[...] + 0.1 * user_v[...]
         for k in range(1, RING):
@@ -225,8 +237,8 @@
 
     for grads in grads_back:
         grads.wait_recv()
-    item_grad = grad_in[0].astype(f32) + grad_in[1].astype(f32) + 0.1 * item_v[...]
-    new_items, _ = adagrad(item_v[...], iacc_v[...], item_grad)
+    whole = grad_in[0].astype(f32) + grad_in[1].astype(f32) + 0.1 * item_v[...]
+    new_items, _ = adagrad(item_v[...], iacc_v[...], whole)
     items_o[...] = new_items
 
     for sent in [swap_items, swap_mask, swap_grad, swap_late, *swap_rates, *items_on, *grads_back]:
@@ -235,6 +247,11 @@
         for k in range(1, RING):
             spread(s, k).wait_send()
             collect(s, k).wait_send()
+
+
+def hand_over(users_i, items_i, users_o, items_o):
+    users_o[...] = users_i[...]
+    items_o[...] = items_i[...]
 
 
 def solution(mesh):
@@ -248,7 +265,7 @@
         cols = items.shape[0]
         plane = RING * rows
         ring_sems = pltpu.SemaphoreType.DMA((strata, RING))
-        return pl.pallas_call(
+        results = pl.pallas_call(
             functools.partial(kernel, n_user),
             out_shape=(
                 jax.ShapeDtypeStruct((rows, rank), f32),
@@ -270,6 +287,7 @@
                 pltpu.VMEM((cols, rank), f32),
                 pltpu.VMEM((strata, 2 * cols, rank), bf16),
                 pltpu.VMEM((cols, rank), bf16),
+                pltpu.VMEM((cols, rank), f32),
                 pltpu.VMEM((strata, plane, rank), bf16),
                 pltpu.VMEM((plane, 2 * cols), bf16),
                 pltpu.VMEM((rows, rank), f32),
@@ -291,6 +309,10 @@
                 collective_id=0, has_side_effects=True, vmem_limit_bytes=56 * 2**20
             ),
         )(users, user_accum, items, item_accum, ratings, tile_mask)
+        return pl.pallas_call(
+            hand_over,
+            out_shape=tuple(jax.ShapeDtypeStruct(r.shape, r.dtype) for r in results),
+        )(*results)
 
     return jax.shard_map(
         body,

time: 62.8 us -> 59 us (0.939)
  the two profiles are of different devices: /device:TPU:9 before, /device:TPU:119 now
where the time goes in v3:
time: 59 us; the launch traced here: 58.8 us
  Pallas kernels  58.2 us (99%)
  between operations  0.64 us (1%)
    pallas_call x1, Pallas kernels, body(): pl.pallas_call(functools.partial(kernel, n_user), out_shape=(jax.ShapeDty...  56.5 us
    pallas_call x1, Pallas kernels, body(): pl.pallas_call(hand_over, out_shape=tuple((jax.ShapeDtypeStruct(r.shape,...  1.72 us

profile of v3, /device:TPU:119, one launch (start us, length us, event | category | flops | bytes accessed | tf_op | source)
XLA Modules:
  0.0 58.8 jit_solution(2672219448501749433)
XLA Ops:
  0.6 56.5 %shard_map.77 = (f32[64,256]{1,0:T(8,128)}, f32[256,256]{1,0:T(8,128)}) custom-call(f32[64,256]{1,0:T(8,128)} %users_h.1, f32[64,256]{1,0:T(8,128)} %uacc_h.1, f32[256,256]{1,0:T(8,128)} %items_h.1, f32[256,256]{1,0:T(8,128)} %iacc_h.1, s32[2,1024,256]{2,1,0:T(8,128)} %rates_h.1, s32[2,2,8]{2,1,0:T(2,128)} %bitcast.1), custom_call_target="tpu_custom_call" | custom-call | tf_op jit(solution)/shard_map/pallas_call | solution.py:268
  57.1 1.7 %shard_map.78 = (f32[64,256]{1,0:T(8,128)}, f32[256,256]{1,0:T(8,128)}) custom-call(f32[64,256]{1,0:T(8,128)} %get-tuple-element.4.users_i, f32[256,256]{1,0:T(8,128)} %get-tuple-element.5.items_i), custom_call_target="tpu_custom_call" | custom-call | tf_op jit(solution)/shard_map/pallas_call | solution.py:312

commit v4 on v3

--- a/solution.py
+++ b/solution.py
@@ -73,13 +73,12 @@
         (half(1, y), rates.at[1]),
     ]
     loads = [pltpu.make_async_copy(src, dst, load_sem.at[k]) for k, (src, dst) in enumerate(loads)]
-    for load in loads:
-        load.start()
-
     near = [forth(k) for k in range(1, RING)] + [(v, j) for v in (after, before) for j in (i, across)] + [(u, across)]
     barrier = pltpu.get_barrier_semaphore()
     for there in near:
         pl.semaphore_signal(barrier, inc=1, device_id=there, device_id_type=MESH)
+    for k in (0, 2, 1, *range(3, len(loads))):
+        loads[k].start()
 
     def copy(src, dst, send, recv, there):
         return pltpu.make_async_remote_copy(
@@ -157,17 +156,17 @@
     gather[0, slot(0), :] = user_v[...].astype(bf16)
     loads[2].wait()
     item_b[0, pl.ds(0, cols), :] = item_v[...].astype(bf16)
-    loads[1].wait()
-    pack_rates(0)
-    loads[4].wait()
     pl.semaphore_wait(barrier, len(near))
 
     for s in range(strata):
         for k in SENDS:
             spread(s, k).start()
         if s == 0:
+            swap_items.start()
+            loads[4].wait()
             swap_mask.start()
-            swap_items.start()
+            loads[1].wait()
+            pack_rates(0)
             for swap in swap_rates:
                 swap.start()
             loads[6].wait()

time: 59 us -> 58.9 us (level)
  no operation moved by 1% of the time
where the time goes in v4:
time: 58.9 us; the launch traced here: 58.7 us
  Pallas kernels  58.1 us (99%)
  between operations  0.64 us (1%)
    pallas_call x1, Pallas kernels, body(): pl.pallas_call(functools.partial(kernel, n_user), out_shape=(jax.ShapeDty...  56.3 us
    pallas_call x1, Pallas kernels, body(): pl.pallas_call(hand_over, out_shape=tuple((jax.ShapeDtypeStruct(r.shape,...  1.72 us

profile of v4, /device:TPU:119, one launch (start us, length us, event | category | flops | bytes accessed | tf_op | source)
XLA Modules:
  0.0 58.7 jit_solution(12601291017781930550)
XLA Ops:
  0.6 56.3 %shard_map.77 = (f32[64,256]{1,0:T(8,128)}, f32[256,256]{1,0:T(8,128)}) custom-call(f32[64,256]{1,0:T(8,128)} %users_h.1, f32[64,256]{1,0:T(8,128)} %uacc_h.1, f32[256,256]{1,0:T(8,128)} %items_h.1, f32[256,256]{1,0:T(8,128)} %iacc_h.1, s32[2,1024,256]{2,1,0:T(8,128)} %rates_h.1, s32[2,2,8]{2,1,0:T(2,128)} %bitcast.1), custom_call_target="tpu_custom_call" | custom-call | tf_op jit(solution)/shard_map/pallas_call | solution.py:267
  57.0 1.7 %shard_map.78 = (f32[64,256]{1,0:T(8,128)}, f32[256,256]{1,0:T(8,128)}) custom-call(f32[64,256]{1,0:T(8,128)} %get-tuple-element.4.users_i, f32[256,256]{1,0:T(8,128)} %get-tuple-element.5.items_i), custom_call_target="tpu_custom_call" | custom-call | tf_op jit(solution)/shard_map/pallas_call | solution.py:311
